TPU v7x, 32 devices: a whole 2x2x4 slice. The times are simulated.
32 devices in a mesh: cls: 4 (over z), col: 8 (over y, x, core).
Axes of the slice: x: 2, y: 2, z: 4, core: 2. Of those that a mesh axis runs over, the one named last changes fastest.
Arguments:
- coeffs_t: float32 [49152, 1024], P(('cls', 'col')), may hold values from -6 to 6
- alpha_table: float32 [64, 4096], replicated, may hold values from -0.1875 to 0.1875
- alpha_blocks: int32 [16, 16], replicated, may hold values from 0 to 15, all different within a row
- alpha_types: int32 [16, 16], replicated, may hold values from 0 to 63
- beta_table: float32 [64, 4096], replicated, may hold values from -0.21875 to 0.21875
- beta_blocks: int32 [768, 12], P('cls'), may hold values from 0 to 383, all different within a row
- beta_types: int32 [768, 12], P('cls'), may hold values from 0 to 63
- row_counts: int32 [8], replicated, may hold values from 1 to 192, 1024 in all
Outputs:
- sigma_slots: float32 [1536, 49152], P('col', 'cls')
Inputs may be any that keep to these rules, and one draw needn't show every extreme that they name: `alpha_blocks`: each row names 16 different alpha blocks. `beta_blocks`: each row names 12 different entries: below 192 a block of the own class, from 192 on a block of the partner class. `row_counts`: the counts sum to 1024 and the largest is exactly 192.
All inputs are finite; a program needn't handle non-finite values.
Results may differ from a plain program's by a relative error of at most 0.0003.
Values sent between devices are 32-bit elements; how exact they have to be, the bound alone decides.
A program may use at most 128 MiB of HBM per device.

v0:
```python
import jax
import jax.numpy as jnp
from jax import lax
from jax.sharding import PartitionSpec as P

exact_mode = lax.Precision.HIGHEST


def swapped(block, axis, apart):
    count = lax.axis_size(axis)
    route = []
    for low in range(count):
        high = low | 1 << apart
        if high != low and high < count:
            route += [(low, high), (high, low)]
    return lax.ppermute(block, axis, route)


def alpha_local(coeffs_t, alpha_table, alpha_blocks, alpha_types):
    alpha_count = alpha_blocks.shape[0]
    block_size = coeffs_t.shape[1] // alpha_count
    column_count = coeffs_t.shape[0]
    blocked = coeffs_t.reshape(column_count, alpha_count, block_size)

    def alpha_add_term(running, column):
        block_ids, type_ids = column
        source = jnp.take(blocked, block_ids, axis=1)
        matrices = jnp.take(alpha_table, type_ids, axis=0).reshape(
            alpha_count, block_size, block_size
        )
        return (running + jnp.einsum("rib,iab->ria", source, matrices, precision=exact_mode), None)

    running, unused = lax.scan(
        alpha_add_term, jnp.zeros(blocked.shape, jnp.float32), (alpha_blocks.T, alpha_types.T)
    )
    return running.reshape(coeffs_t.shape)


def beta_local(own_rows, partner_rows, beta_table, beta_blocks, beta_types):
    row_total = own_rows.shape[0]
    class_width = own_rows.shape[1]
    block_size = beta_blocks.shape[0] * 0 + int(round(beta_table.shape[1] ** 0.5))
    per_class = class_width // block_size
    stacked = jnp.concatenate([own_rows, partner_rows], 1).reshape(
        row_total, 2 * per_class, block_size
    )

    def beta_add_term(running, column):
        block_ids, type_ids = column
        source = jnp.take(stacked, block_ids, axis=1)
        matrices = jnp.take(beta_table, type_ids, axis=0).reshape(per_class, block_size, block_size)
        return (running + jnp.einsum("rma,mab->rmb", source, matrices, precision=exact_mode), None)

    initial = jnp.zeros((row_total, per_class, block_size), jnp.float32)
    running, unused = lax.scan(beta_add_term, initial, (beta_blocks.T, beta_types.T))
    return running.reshape(row_total, class_width)


def gather_slots(local_t, starts, row_counts, capacity):
    padded = jnp.concatenate([local_t, jnp.zeros((local_t.shape[0], capacity), local_t.dtype)], 1)
    offsets = jnp.arange(capacity, dtype=jnp.int32)
    row_index = starts[:, None] + offsets[None, :]
    in_range = offsets[None, :] < row_counts[:, None]
    picked = jnp.take(padded, row_index, axis=1)
    picked = jnp.where(in_range[None, :, :], picked, jnp.float32(0.0))
    return jnp.transpose(picked, (1, 2, 0))


def on_device(
    coeffs_t,
    alpha_table,
    alpha_blocks,
    alpha_types,
    beta_table,
    beta_blocks,
    beta_types,
    row_counts,
):
    groups = lax.axis_size("col")
    capacity = 3 * coeffs_t.shape[1] // (2 * groups)
    starts = jnp.cumsum(row_counts) - row_counts
    alpha_part = alpha_local(coeffs_t, alpha_table, alpha_blocks, alpha_types)
    coeff_slots = gather_slots(coeffs_t, starts, row_counts, capacity)
    alpha_slots = gather_slots(alpha_part, starts, row_counts, capacity)
    partner_cols = swapped(coeffs_t, "cls", 0)
    partner_slots = gather_slots(partner_cols, starts, row_counts, capacity)
    own_rows, alpha_rows, partner_rows = (
        lax.all_to_all(coeff_slots, "col", split_axis=0, concat_axis=2, tiled=True),
        lax.all_to_all(alpha_slots, "col", split_axis=0, concat_axis=2, tiled=True),
        lax.all_to_all(partner_slots, "col", split_axis=0, concat_axis=2, tiled=True),
    )
    own_rows = own_rows.reshape(capacity, -1)
    partner_rows = partner_rows.reshape(capacity, -1)
    alpha_rows = alpha_rows.reshape(capacity, -1)
    return alpha_rows + beta_local(own_rows, partner_rows, beta_table, beta_blocks, beta_types)


def solution(mesh):
    return jax.shard_map(
        on_device,
        mesh=mesh,
        in_specs=(P(("cls", "col"), None), P(), P(), P(), P(), P("cls", None), P("cls", None), P()),
        out_specs=P("col", "cls"),
        check_vma=False,
    )
```

profile of v0, /device:TPU:0, one launch (start us, length us, event | category | flops | bytes accessed | tf_op | source)
XLA Modules:
  0.0 1387.6 jit_solution(9231187841385495843)
XLA Ops:
  9.9 283.2 %while.22 = (s32[]{:T(128)}, f32[1536,16,64]{0,2,1:T(8,128)}, s32[16,16]{1,0:T(8,128)S(1)}, f32[64,4096]{1,0:T(8,128)S(1)}, s32[16,16]{1,0:T(8,128)S(1)}, /*index=5*/f32[1536,16,64]{0,2,1:T(8,128)}, s32[]{:T(128)}, s32[]{:T(128)}) while((s32[]{:T(128)}, f32[1536,16,64]{0,2,1:T(8,128)}, s32[16,16]{1,0:T(8,128)S(1)}, ...), condition=%wide.region_1.2_spmd.clone, body=%wide.region_0.0_spmd.clone.sunk | while | flops 1212745984 | bytes 32776996 | solution.py:33
  317.2 13.5 gather_fusion.5
  350.6 18.2 %fusion.23 = (f32[8,192,1536]{2,1,0:T(8,128)}, f32[8,192,1536]{2,1,0:T(8,128)S(1)}, f32[8,192,1536]{2,1,0:T(8,128)}) fusion(f32[8,192,1536]{2,1,0:T(8,128)} %bitcast.117, pred[8,192]{1,0:T(8,128)(4,1)S(1)} %get-tuple-element.152, pred[8,192]{1,0:T(8,128)(4,1)S(1)} %get-tuple-element.151, f32[8,192,1536]{2,1,0:T(8,128)} %bitcast.118, f32[8,192,1536]{2,1,0:T(8,128)} %bitcast.119), kind=kLoop, calls=%fused_computation.54 | loop fusion | flops 14155776 | bytes 56626176 | tf_op jit(solution)/shard_map/transpose | solution.py:66
  368.8 108.9 %all_to_all.45 = f32[8,192,1536]{2,1,0:T(8,128)} all-to-all(f32[8,192,1536]{2,1,0:T(8,128)S(1)} %get-tuple-element.149), channel_id=1, replica_groups=mesh['cls'=4,'col'=8] {'col'}, dimensions={0} | all-to-all | bytes 18874368 | tf_op jit(solution)/shard_map/all_to_all | solution.py:88
  494.2 93.8 %all-to-all-done.2 = f32[8,192,1536]{2,1,0:T(8,128)} async-done(((f32[8,192,1536]{2,1,0:T(8,128)}), f32[8,192,1536]{2,1,0:T(8,128)}, u32[]{:S(2)}, u32[]{:S(2)}) %all-to-all-start.2) | async-done | bytes 9437216 | tf_op jit(solution)/shard_map/all_to_all | solution.py:90
  604.6 18.5 %pad_maximum_fusion = f32[192,384,64]{0,2,1:T(8,128)} fusion(f32[192,192,64]{0,2,1:T(8,128)} %bitcast.121, f32[192,192,64]{0,2,1:T(8,128)} %bitcast.120), kind=kLoop, calls=%fused_computation.47 | loop fusion | flops 4718592 | bytes 37748736 | tf_op jit(solution)/shard_map/concatenate | solution.py:44
  623.1 727.6 %while.23 = (s32[]{:T(128)}, f32[192,192,64]{0,2,1:T(8,128)}, s32[12,192]{1,0:T(8,128)}, f32[64,4096]{1,0:T(8,128)S(1)}, s32[12,192]{1,0:T(8,128)}, /*index=5*/f32[192,384,64]{0,2,1:T(8,128)}, s32[]{:T(128)}, s32[]{:T(128)}) while((s32[]{:T(128)}, f32[192,192,64]{0,2,1:T(8,128)}, s32[12,192]{1,0:T(8,128)}, ...), condition=%wide.region_4.6_spmd.clone, body=%wide.region_3.5_spmd.clone.sunk | while | flops 1819809152 | bytes 75515744 | solution.py:55
  644.2 18.8 %gather_fusion.3 = f32[192,192,64]{1,2,0:T(8,128)} fusion(f32[192,384,64]{0,2,1:T(8,128)} %get-tuple-element.288, s32[1024]{0:T(1024)S(1)} %pad_clamp_fusion.12), kind=kCustom, calls=%fused_computation.4.clone.clone.1 | custom fusion | bytes 18875136 | tf_op jit(solution)/shard_map/while/body/eval_jaxpr/jit(_take)/gather | solution.py:50
  663.0 19.1 %bitcast_add_fusion.6 = f32[192,192,64]{0,2,1:T(8,128)} fusion(f32[192,192,64]{0,2,1:T(8,128)} %get-tuple-element.276, pred[]{:T(512)S(6)} %compare.10, f32[192,64,64]{1,2,0:T(8,128)} %copy.45, f32[192,192,64]{1,2,0:T(8,128)} %gather_fusion.3, pred[192]{0:T(512)(128)(4,1)S(1)} %compare_and_fusion.10), kind=kOutput, calls=%fused_computation.29.clone.1 | convolution fusion | flops 1819017216 | bytes 31457472 | tf_op jit(solution)/shard_map/while/body/eval_jaxpr/rma,mab->rmb/dot_general | solution.py:52
  703.1 18.8 %gather_fusion.3 = f32[192,192,64]{1,2,0:T(8,128)} fusion(f32[192,384,64]{0,2,1:T(8,128)} %get-tuple-element.288, s32[1024]{0:T(1024)S(1)} %pad_clamp_fusion.12), kind=kCustom, calls=%fused_computation.4.clone.clone.1 | custom fusion | bytes 18875136 | tf_op jit(solution)/shard_map/while/body/eval_jaxpr/jit(_take)/gather | solution.py:50
  721.9 20.8 %bitcast_add_fusion.6 = f32[192,192,64]{0,2,1:T(8,128)} fusion(f32[192,192,64]{0,2,1:T(8,128)} %get-tuple-element.276, pred[]{:T(512)S(6)} %compare.10, f32[192,64,64]{1,2,0:T(8,128)} %copy.45, f32[192,192,64]{1,2,0:T(8,128)} %gather_fusion.3, pred[192]{0:T(512)(128)(4,1)S(1)} %compare_and_fusion.10), kind=kOutput, calls=%fused_computation.29.clone.1 | convolution fusion | flops 1819017216 | bytes 31457472 | tf_op jit(solution)/shard_map/while/body/eval_jaxpr/rma,mab->rmb/dot_general | solution.py:52
  763.9 18.8 %gather_fusion.3 = f32[192,192,64]{1,2,0:T(8,128)} fusion(f32[192,384,64]{0,2,1:T(8,128)} %get-tuple-element.288, s32[1024]{0:T(1024)S(1)} %pad_clamp_fusion.12), kind=kCustom, calls=%fused_computation.4.clone.clone.1 | custom fusion | bytes 18875136 | tf_op jit(solution)/shard_map/while/body/eval_jaxpr/jit(_take)/gather | solution.py:50
  782.7 20.9 %bitcast_add_fusion.6 = f32[192,192,64]{0,2,1:T(8,128)} fusion(f32[192,192,64]{0,2,1:T(8,128)} %get-tuple-element.276, pred[]{:T(512)S(6)} %compare.10, f32[192,64,64]{1,2,0:T(8,128)} %copy.45, f32[192,192,64]{1,2,0:T(8,128)} %gather_fusion.3, pred[192]{0:T(512)(128)(4,1)S(1)} %compare_and_fusion.10), kind=kOutput, calls=%fused_computation.29.clone.1 | convolution fusion | flops 1819017216 | bytes 31457472 | tf_op jit(solution)/shard_map/while/body/eval_jaxpr/rma,mab->rmb/dot_general | solution.py:52
  824.7 18.8 %gather_fusion.3 = f32[192,192,64]{1,2,0:T(8,128)} fusion(f32[192,384,64]{0,2,1:T(8,128)} %get-tuple-element.288, s32[1024]{0:T(1024)S(1)} %pad_clamp_fusion.12), kind=kCustom, calls=%fused_computation.4.clone.clone.1 | custom fusion | bytes 18875136 | tf_op jit(solution)/shard_map/while/body/eval_jaxpr/jit(_take)/gather | solution.py:50
  843.5 20.9 %bitcast_add_fusion.6 = f32[192,192,64]{0,2,1:T(8,128)} fusion(f32[192,192,64]{0,2,1:T(8,128)} %get-tuple-element.276, pred[]{:T(512)S(6)} %compare.10, f32[192,64,64]{1,2,0:T(8,128)} %copy.45, f32[192,192,64]{1,2,0:T(8,128)} %gather_fusion.3, pred[192]{0:T(512)(128)(4,1)S(1)} %compare_and_fusion.10), kind=kOutput, calls=%fused_computation.29.clone.1 | convolution fusion | flops 1819017216 | bytes 31457472 | tf_op jit(solution)/shard_map/while/body/eval_jaxpr/rma,mab->rmb/dot_general | solution.py:52
  885.5 18.8 %gather_fusion.3 = f32[192,192,64]{1,2,0:T(8,128)} fusion(f32[192,384,64]{0,2,1:T(8,128)} %get-tuple-element.288, s32[1024]{0:T(1024)S(1)} %pad_clamp_fusion.12), kind=kCustom, calls=%fused_computation.4.clone.clone.1 | custom fusion | bytes 18875136 | tf_op jit(solution)/shard_map/while/body/eval_jaxpr/jit(_take)/gather | solution.py:50
  904.3 20.8 %bitcast_add_fusion.6 = f32[192,192,64]{0,2,1:T(8,128)} fusion(f32[192,192,64]{0,2,1:T(8,128)} %get-tuple-element.276, pred[]{:T(512)S(6)} %compare.10, f32[192,64,64]{1,2,0:T(8,128)} %copy.45, f32[192,192,64]{1,2,0:T(8,128)} %gather_fusion.3, pred[192]{0:T(512)(128)(4,1)S(1)} %compare_and_fusion.10), kind=kOutput, calls=%fused_computation.29.clone.1 | convolution fusion | flops 1819017216 | bytes 31457472 | tf_op jit(solution)/shard_map/while/body/eval_jaxpr/rma,mab->rmb/dot_general | solution.py:52
  946.3 18.8 %gather_fusion.3 = f32[192,192,64]{1,2,0:T(8,128)} fusion(f32[192,384,64]{0,2,1:T(8,128)} %get-tuple-element.288, s32[1024]{0:T(1024)S(1)} %pad_clamp_fusion.12), kind=kCustom, calls=%fused_computation.4.clone.clone.1 | custom fusion | bytes 18875136 | tf_op jit(solution)/shard_map/while/body/eval_jaxpr/jit(_take)/gather | solution.py:50
  965.1 20.9 %bitcast_add_fusion.6 = f32[192,192,64]{0,2,1:T(8,128)} fusion(f32[192,192,64]{0,2,1:T(8,128)} %get-tuple-element.276, pred[]{:T(512)S(6)} %compare.10, f32[192,64,64]{1,2,0:T(8,128)} %copy.45, f32[192,192,64]{1,2,0:T(8,128)} %gather_fusion.3, pred[192]{0:T(512)(128)(4,1)S(1)} %compare_and_fusion.10), kind=kOutput, calls=%fused_computation.29.clone.1 | convolution fusion | flops 1819017216 | bytes 31457472 | tf_op jit(solution)/shard_map/while/body/eval_jaxpr/rma,mab->rmb/dot_general | solution.py:52
  1007.1 18.8 %gather_fusion.3 = f32[192,192,64]{1,2,0:T(8,128)} fusion(f32[192,384,64]{0,2,1:T(8,128)} %get-tuple-element.288, s32[1024]{0:T(1024)S(1)} %pad_clamp_fusion.12), kind=kCustom, calls=%fused_computation.4.clone.clone.1 | custom fusion | bytes 18875136 | tf_op jit(solution)/shard_map/while/body/eval_jaxpr/jit(_take)/gather | solution.py:50
  1025.9 20.9 %bitcast_add_fusion.6 = f32[192,192,64]{0,2,1:T(8,128)} fusion(f32[192,192,64]{0,2,1:T(8,128)} %get-tuple-element.276, pred[]{:T(512)S(6)} %compare.10, f32[192,64,64]{1,2,0:T(8,128)} %copy.45, f32[192,192,64]{1,2,0:T(8,128)} %gather_fusion.3, pred[192]{0:T(512)(128)(4,1)S(1)} %compare_and_fusion.10), kind=kOutput, calls=%fused_computation.29.clone.1 | convolution fusion | flops 1819017216 | bytes 31457472 | tf_op jit(solution)/shard_map/while/body/eval_jaxpr/rma,mab->rmb/dot_general | solution.py:52
  1067.8 18.8 %gather_fusion.3 = f32[192,192,64]{1,2,0:T(8,128)} fusion(f32[192,384,64]{0,2,1:T(8,128)} %get-tuple-element.288, s32[1024]{0:T(1024)S(1)} %pad_clamp_fusion.12), kind=kCustom, calls=%fused_computation.4.clone.clone.1 | custom fusion | bytes 18875136 | tf_op jit(solution)/shard_map/while/body/eval_jaxpr/jit(_take)/gather | solution.py:50
  1086.7 20.9 %bitcast_add_fusion.6 = f32[192,192,64]{0,2,1:T(8,128)} fusion(f32[192,192,64]{0,2,1:T(8,128)} %get-tuple-element.276, pred[]{:T(512)S(6)} %compare.10, f32[192,64,64]{1,2,0:T(8,128)} %copy.45, f32[192,192,64]{1,2,0:T(8,128)} %gather_fusion.3, pred[192]{0:T(512)(128)(4,1)S(1)} %compare_and_fusion.10), kind=kOutput, calls=%fused_computation.29.clone.1 | convolution fusion | flops 1819017216 | bytes 31457472 | tf_op jit(solution)/shard_map/while/body/eval_jaxpr/rma,mab->rmb/dot_general | solution.py:52
  1128.6 18.8 %gather_fusion.3 = f32[192,192,64]{1,2,0:T(8,128)} fusion(f32[192,384,64]{0,2,1:T(8,128)} %get-tuple-element.288, s32[1024]{0:T(1024)S(1)} %pad_clamp_fusion.12), kind=kCustom, calls=%fused_computation.4.clone.clone.1 | custom fusion | bytes 18875136 | tf_op jit(solution)/shard_map/while/body/eval_jaxpr/jit(_take)/gather | solution.py:50
  1147.4 20.9 %bitcast_add_fusion.6 = f32[192,192,64]{0,2,1:T(8,128)} fusion(f32[192,192,64]{0,2,1:T(8,128)} %get-tuple-element.276, pred[]{:T(512)S(6)} %compare.10, f32[192,64,64]{1,2,0:T(8,128)} %copy.45, f32[192,192,64]{1,2,0:T(8,128)} %gather_fusion.3, pred[192]{0:T(512)(128)(4,1)S(1)} %compare_and_fusion.10), kind=kOutput, calls=%fused_computation.29.clone.1 | convolution fusion | flops 1819017216 | bytes 31457472 | tf_op jit(solution)/shard_map/while/body/eval_jaxpr/rma,mab->rmb/dot_general | solution.py:52
  1189.4 18.8 %gather_fusion.3 = f32[192,192,64]{1,2,0:T(8,128)} fusion(f32[192,384,64]{0,2,1:T(8,128)} %get-tuple-element.288, s32[1024]{0:T(1024)S(1)} %pad_clamp_fusion.12), kind=kCustom, calls=%fused_computation.4.clone.clone.1 | custom fusion | bytes 18875136 | tf_op jit(solution)/shard_map/while/body/eval_jaxpr/jit(_take)/gather | solution.py:50
  1208.2 20.9 %bitcast_add_fusion.6 = f32[192,192,64]{0,2,1:T(8,128)} fusion(f32[192,192,64]{0,2,1:T(8,128)} %get-tuple-element.276, pred[]{:T(512)S(6)} %compare.10, f32[192,64,64]{1,2,0:T(8,128)} %copy.45, f32[192,192,64]{1,2,0:T(8,128)} %gather_fusion.3, pred[192]{0:T(512)(128)(4,1)S(1)} %compare_and_fusion.10), kind=kOutput, calls=%fused_computation.29.clone.1 | convolution fusion | flops 1819017216 | bytes 31457472 | tf_op jit(solution)/shard_map/while/body/eval_jaxpr/rma,mab->rmb/dot_general | solution.py:52
  1250.2 18.8 %gather_fusion.3 = f32[192,192,64]{1,2,0:T(8,128)} fusion(f32[192,384,64]{0,2,1:T(8,128)} %get-tuple-element.288, s32[1024]{0:T(1024)S(1)} %pad_clamp_fusion.12), kind=kCustom, calls=%fused_computation.4.clone.clone.1 | custom fusion | bytes 18875136 | tf_op jit(solution)/shard_map/while/body/eval_jaxpr/jit(_take)/gather | solution.py:50
  1269.0 20.9 %bitcast_add_fusion.6 = f32[192,192,64]{0,2,1:T(8,128)} fusion(f32[192,192,64]{0,2,1:T(8,128)} %get-tuple-element.276, pred[]{:T(512)S(6)} %compare.10, f32[192,64,64]{1,2,0:T(8,128)} %copy.45, f32[192,192,64]{1,2,0:T(8,128)} %gather_fusion.3, pred[192]{0:T(512)(128)(4,1)S(1)} %compare_and_fusion.10), kind=kOutput, calls=%fused_computation.29.clone.1 | convolution fusion | flops 1819017216 | bytes 31457472 | tf_op jit(solution)/shard_map/while/body/eval_jaxpr/rma,mab->rmb/dot_general | solution.py:52
  1311.0 18.8 %gather_fusion.3 = f32[192,192,64]{1,2,0:T(8,128)} fusion(f32[192,384,64]{0,2,1:T(8,128)} %get-tuple-element.288, s32[1024]{0:T(1024)S(1)} %pad_clamp_fusion.12), kind=kCustom, calls=%fused_computation.4.clone.clone.1 | custom fusion | bytes 18875136 | tf_op jit(solution)/shard_map/while/body/eval_jaxpr/jit(_take)/gather | solution.py:50
  1329.8 20.8 %bitcast_add_fusion.6 = f32[192,192,64]{0,2,1:T(8,128)} fusion(f32[192,192,64]{0,2,1:T(8,128)} %get-tuple-element.276, pred[]{:T(512)S(6)} %compare.10, f32[192,64,64]{1,2,0:T(8,128)} %copy.45, f32[192,192,64]{1,2,0:T(8,128)} %gather_fusion.3, pred[192]{0:T(512)(128)(4,1)S(1)} %compare_and_fusion.10), kind=kOutput, calls=%fused_computation.29.clone.1 | convolution fusion | flops 1819017216 | bytes 31457472 | tf_op jit(solution)/shard_map/while/body/eval_jaxpr/rma,mab->rmb/dot_general | solution.py:52
  1362.1 13.9 %bitcast_add_fusion.2 = f32[192,12288]{0,1:T(8,128)} fusion(f32[192,192,64]{0,2,1:T(8,128)} %get-tuple-element.71, f32[1,192,8,1536]{1,3,2,0:T(8,128)} %copy.36), kind=kLoop, calls=%fused_computation.48 | loop fusion | flops 2359296 | bytes 28311552 | tf_op jit(solution)/shard_map/add | solution.py:95
  (276 shorter events, 645.8 us)
Async XLA Ops:
  0.0 9.8 copy-start.2
  0.0 9.8 copy-start.3
  0.0 9.9 copy-start.1
  6.7 324.0 %collective-permute-start = (f32[1536,1024]{0,1:T(8,128)}, f32[1536,1024]{0,1:T(8,128)}, u32[]{:S(2)}, u32[]{:S(2)}) collective-permute-start(f32[1536,1024]{0,1:T(8,128)} %copy.35), channel_id=1, source_target_pairs={{0,8},{8,0},{16,24},{24,16},{1,9},{9,1},{17,25},{25,17},{2,10},{10... | collective-permute-start | bytes 18874376 | tf_op jit(solution)/shard_map/ppermute | solution.py:16
  9.9 283.2 %copy-start.4 = (s32[8]{0:T(128)S(1)}, s32[8]{0:T(128)}, u32[]{:S(2)}) copy-start(s32[8]{0:T(128)} %param.21) | copy-start | bytes 100
  293.1 6.9 slice-start
  293.5 6.6 slice-start.1
  477.7 110.4 %all-to-all-start.2 = ((f32[8,192,1536]{2,1,0:T(8,128)}), f32[8,192,1536]{2,1,0:T(8,128)}, u32[]{:S(2)}, u32[]{:S(2)}) async-start(f32[8,192,1536]{2,1,0:T(8,128)} %get-tuple-element.150), calls=%async_computation.2 | async-start | bytes 18874368 | tf_op jit(solution)/shard_map/all_to_all | solution.py:90
  588.0 762.6 %all-to-all-start = ((f32[8,192,1536]{2,1,0:T(8,128)}), f32[8,192,1536]{2,1,0:T(8,128)}, u32[]{:S(2)}, u32[]{:S(2)}) async-start(f32[8,192,1536]{2,1,0:T(8,128)} %get-tuple-element.148), calls=%async_computation | async-start | bytes 18874368 | tf_op jit(solution)/shard_map/all_to_all | solution.py:89
  604.6 18.5 %copy-start = (f32[64,4096]{1,0:T(8,128)S(1)}, f32[64,4096]{1,0:T(8,128)}, u32[]{:S(2)}) copy-start(f32[64,4096]{1,0:T(8,128)} %param.18) | copy-start | bytes 3145732
where the time goes:
time: 1390 us
  local copies, waits for them, and re-layouts  639 us (46%)
  matrix products  415 us (30%)
  other arithmetic  118 us (8%)
  blocking collectives  109 us (8%)
  waiting for transfers between devices  93.8 us (7%)
    dot_general x12, matrix products, beta_add_term(): jnp.einsum('rma,mab->rmb', source, matrices, precision=exact_mode)  249 us
    gather x12, local copies, waits for them, and re-layouts, beta_add_term(): source = jnp.take(stacked, block_ids, axis=1)  226 us
    dot_general x16, matrix products, alpha_add_term(): jnp.einsum('rib,iab->ria', source, matrices, precision=exact_mode)  166 us
    all_to_all x1, blocking collectives, on_device(): lax.all_to_all(coeff_slots, 'col', split_axis=0, concat_axis=2, tiled=True)  109 us
    gather x16, local copies, waits for them, and re-layouts, alpha_add_term(): source = jnp.take(blocked, block_ids, axis=1)  102 us
    gather x24, local copies, waits for them, and re-layouts, beta_add_term(): jnp.take(beta_table, type_ids, axis=0)  101 us
    all_to_all x1, waiting for transfers between devices, on_device(): lax.all_to_all(partner_slots, 'col', split_axis=0, concat_axis=2, tiled=T...  93.8 us
    select_n x12, local copies, waits for them, and re-layouts, beta_add_term(): jnp.take(beta_table, type_ids, axis=0)  86.5 us
  transfers between devices with their start and end apart: 3, of which 1 were waited for; matrix products, arithmetic and copies ran while one was open for 79% of the time, Pallas kernels for 0%

commit v1 on v0

v1 whole, which is shorter than its diff:
```python
import functools

import jax
import jax.numpy as jnp
from jax import lax
from jax.experimental import pallas as pl
from jax.experimental.pallas import tpu as pltpu
from jax.sharding import PartitionSpec as P

ROW_PARTS = 3
TILE = 8
VMEM_BYTES = 56 * 1024 * 1024


def swapped(block, axis, apart):
    count = lax.axis_size(axis)
    route = []
    for low in range(count):
        high = low | 1 << apart
        if high != low and high < count:
            route += [(low, high), (high, low)]
    return lax.ppermute(block, axis, route)


def split_outside(x):
    high = lax.reduce_precision(x, 8, 7)
    return high.astype(jnp.bfloat16), (x - high).astype(jnp.bfloat16)


def split_inside(x):
    high = x.astype(jnp.bfloat16)
    return high, (x - high.astype(jnp.float32)).astype(jnp.bfloat16)


def column_chunk(width):
    for chunk in (512, 384, 256, 128):
        if width % chunk == 0:
            return chunk
    return width


def write_slots(starts, tall, out_refs):
    parts = len(out_refs)
    piece = out_refs[0].shape[1]
    for slot in range(out_refs[0].shape[0]):
        for part in range(parts):
            first = starts[slot] + part * piece
            shift = lax.rem(first, TILE)
            span = piece + TILE
            rows = pl.ds(pl.multiple_of(first - shift, TILE), span)
            moved = pltpu.roll(tall[rows, :], lax.rem(span - shift, span), 0)
            out_refs[part][slot] = moved[:piece]


def coeff_kernel(starts, coeffs, *rest):
    out_refs, tall = rest[:-1], rest[-1]
    rows = coeffs.shape[1]
    tall[:rows, :] = coeffs[...].T
    tall[rows:, :] = jnp.zeros((tall.shape[0] - rows, tall.shape[1]), jnp.float32)
    write_slots(starts, tall, out_refs)


def alpha_kernel(starts, coeffs, high_ref, low_ref, out_ref, tall):
    rows = coeffs.shape[1]
    c_high, c_low = split_inside(coeffs[...])
    dot = functools.partial(
        lax.dot_general,
        dimension_numbers=(((1,), (1,)), ((), ())),
        preferred_element_type=jnp.float32,
    )
    tall[:rows, :] = (dot(low_ref[...], c_high) + dot(high_ref[...], c_low)) + dot(
        high_ref[...], c_high
    )
    tall[rows:, :] = jnp.zeros((tall.shape[0] - rows, tall.shape[1]), jnp.float32)
    write_slots(starts, tall, [out_ref])


def slots_call(kernel, coeffs_t, starts, matrices, groups, capacity, parts, name):
    width, rows = coeffs_t.shape
    chunk = column_chunk(width)
    piece = capacity // parts
    out = jax.ShapeDtypeStruct((groups, piece, width), jnp.float32)
    return pl.pallas_call(
        kernel,
        out_shape=[out] * parts,
        grid=(width // chunk,),
        in_specs=[
            pl.BlockSpec(memory_space=pltpu.SMEM),
            pl.BlockSpec((chunk, rows), lambda i: (i, 0)),
        ]
        + [pl.BlockSpec(m.shape, lambda i: (0, 0)) for m in matrices],
        out_specs=[pl.BlockSpec((groups, piece, chunk), lambda i: (0, 0, i))] * parts,
        scratch_shapes=[pltpu.VMEM((rows + capacity + TILE, chunk), jnp.float32)],
        compiler_params=pltpu.CompilerParams(vmem_limit_bytes=VMEM_BYTES),
        name=name,
    )(starts, coeffs_t, *matrices)


def beta_kernel(steps, parts, block, keep, entries, types, *rest):
    own, partner = rest[:parts], rest[parts : 2 * parts]
    alpha, left, right, out, x_high, x_low = rest[2 * parts :]
    step = pl.program_id(0)
    width = alpha.shape[2]
    per_row = entries.shape[0] // (x_high.shape[0] // (2 * block))

    def store(pieces, at):
        tall = jnp.concatenate([piece[0] for piece in pieces], 0) if parts > 1 else pieces[0][0]
        high, low = split_inside(tall.T)
        rows = pl.ds(pl.multiple_of(at * width, block), width)
        x_high[rows, :] = high
        x_low[rows, :] = low

    @pl.when(step < steps)
    def _():
        store(own, step)

    @pl.when(jnp.logical_and(step >= steps, step < 2 * steps))
    def _():
        store(partner, step)

    def one(m):
        base = m * per_row
        places = [
            pl.ds(pl.multiple_of(entries[base + k] * block, block), block) for k in range(per_row)
        ]
        weights = jnp.concatenate(
            [
                left[types[base + k]] + right[types[base + k + 1]]
                for k in range(0, per_row, 2)
            ],
            1,
        )
        high = jnp.concatenate([x_high[place, :] for place in places], 0)
        low = jnp.concatenate([x_low[place, :] for place in places], 0)
        both = jnp.dot(weights, high, preferred_element_type=jnp.float32)
        cross = jnp.dot(weights[:block], low, preferred_element_type=jnp.float32)
        return both[:block] + (both[block:] + cross)

    @pl.when(step >= 2 * steps)
    def _():
        first = (step - 2 * steps) * (width // block)
        row = lax.broadcasted_iota(jnp.int32, (out.shape[0], 2 * block), 0)
        kept = row < keep[0]

        def pair(at, carry):
            m = first + 2 * at
            tall = jnp.concatenate([one(m), one(m + 1)], 0)
            lanes = pl.ds(pl.multiple_of(at * (2 * block), 2 * block), 2 * block)
            total = tall.T + alpha[0, :, lanes]
            out[:, lanes] = jnp.where(kept, total, jnp.float32(0.0))
            return carry

        lax.fori_loop(0, width // (2 * block), pair, 0)


def beta_call(own, partner, alpha, left, right, entries, types, keep, block):
    groups, capacity, width = alpha.shape
    parts = len(own)
    piece = capacity // parts
    whole = lambda a: pl.BlockSpec(a.shape, lambda i: (0, 0, 0))
    smem = pl.BlockSpec(memory_space=pltpu.SMEM)

    def at(offset):
        return lambda i: (jnp.clip(i - offset, 0, groups - 1), 0, 0)

    return pl.pallas_call(
        functools.partial(beta_kernel, groups, parts, block),
        out_shape=jax.ShapeDtypeStruct((capacity, groups * width), jnp.float32),
        grid=(3 * groups,),
        in_specs=[smem, smem, smem]
        + [pl.BlockSpec((1, piece, width), at(0))] * parts
        + [pl.BlockSpec((1, piece, width), at(groups))] * parts
        + [pl.BlockSpec((1, capacity, width), at(2 * groups)), whole(left), whole(right)],
        out_specs=pl.BlockSpec(
            (capacity, width), lambda i: (0, jnp.clip(i - 2 * groups, 0, groups - 1))
        ),
        scratch_shapes=[pltpu.VMEM((2 * groups * width, capacity), jnp.bfloat16)] * 2,
        compiler_params=pltpu.CompilerParams(vmem_limit_bytes=VMEM_BYTES),
        name="beta_sum",
    )(keep, entries, types, *own, *partner, alpha, left, right)


def alpha_matrix(alpha_table, alpha_blocks, alpha_types, block):
    count = alpha_blocks.shape[0]
    hit = alpha_blocks[:, :, None] == jnp.arange(count, dtype=jnp.int32)[None, None, :]
    type_of = jnp.sum(jnp.where(hit, alpha_types[:, :, None], 0), 1)
    matrices = jnp.take(alpha_table, type_of, axis=0)
    matrices = jnp.where(jnp.any(hit, 1)[:, :, None], matrices, jnp.float32(0.0))
    matrices = matrices.reshape(count, count, block, block)
    return jnp.transpose(matrices, (0, 2, 1, 3)).reshape(count * block, count * block)


def beta_weights(beta_table, block):
    tables = jnp.transpose(beta_table.reshape(-1, block, block), (0, 2, 1))
    both = jnp.concatenate(split_outside(tables), 1)
    return (
        jnp.pad(both, ((0, 0), (0, 0), (0, block))),
        jnp.pad(both, ((0, 0), (0, 0), (block, 0))),
    )


def even_wide(x, block):
    groups, rows, width = x.shape
    if width % (2 * block) == 0:
        return x
    x = x.reshape(groups // 2, 2, rows, width)
    return jnp.transpose(x, (0, 2, 1, 3)).reshape(groups // 2, rows, 2 * width)


def on_device(
    coeffs_t,
    alpha_table,
    alpha_blocks,
    alpha_types,
    beta_table,
    beta_blocks,
    beta_types,
    row_counts,
):
    groups = lax.axis_size("col")
    rows = coeffs_t.shape[1]
    capacity = 3 * rows // (2 * groups)
    block = rows // alpha_blocks.shape[0]
    starts = (jnp.cumsum(row_counts) - row_counts).astype(jnp.int32)
    keep = lax.dynamic_slice(row_counts, (lax.axis_index("col"),), (1,))

    coeff_slots = slots_call(
        coeff_kernel, coeffs_t, starts, (), groups, capacity, ROW_PARTS, "coeff_slots"
    )
    own, partner = [], []
    for part in coeff_slots:
        got = lax.all_to_all(part, "col", split_axis=0, concat_axis=0, tiled=True)
        own.append(got)
        partner.append(swapped(got, "cls", 0))
    matrix = split_outside(alpha_matrix(alpha_table, alpha_blocks, alpha_types, block))
    (alpha_slots,) = slots_call(
        alpha_kernel, coeffs_t, starts, matrix, groups, capacity, 1, "alpha_slots"
    )
    alpha = lax.all_to_all(alpha_slots, "col", split_axis=0, concat_axis=0, tiled=True)
    left, right = beta_weights(beta_table, block)
    wide = lambda x: even_wide(x, block)
    return beta_call(
        [wide(x) for x in own],
        [wide(x) for x in partner],
        wide(alpha),
        left,
        right,
        beta_blocks.reshape(-1),
        beta_types.reshape(-1),
        keep,
        block,
    )


def solution(mesh):
    return jax.shard_map(
        on_device,
        mesh=mesh,
        in_specs=(P(("cls", "col"), None), P(), P(), P(), P(), P("cls", None), P("cls", None), P()),
        out_specs=P("col", "cls"),
        check_vma=False,
    )
```

time: 1390 us -> 435 us (0.31)
  local copies, waits for them, and re-layouts: 639 us -> 29.2 us
  matrix products: 415 us -> 0 us
  waiting for transfers between devices: 93.8 us -> 191 us
  other arithmetic: 118 us -> 23.2 us
  Pallas kernels: 0 us -> 92.3 us
  blocking collectives: 109 us -> 84.4 us
    gather x87 -> x2, local copies, waits for them, and re-layouts: 483 us -> 11.7 us  [alpha_matrix(): matrices = jnp.take(alpha_table, type_of, axis=0)]
    dot_general x28 -> x0, matrix products: 415 us -> none  [the longest x12 249 us: beta_add_term(): jnp.einsum('rma,mab->rmb', source, matrices, precision=exact_mode)]
    ppermute x1 -> x3, waiting for transfers between devices: 0.01 us -> 191 us  [swapped(): return lax.ppermute(block, axis, route)]
    all_to_all x2, waiting for transfers between devices: 93.8 us -> 0.01 us  [the longest x1 0.01 us: on_device(): got = lax.all_to_all(part, 'col', split_axis=0, concat_axis=0, tiled=True)]
    pallas_call x0 -> x3, Pallas kernels: none -> 92.3 us  [the longest x1 65.2 us: beta_call(): pl.pallas_call(functools.partial(beta_kernel, groups, parts, block), out_...]
    select_n x12 -> x1, local copies, waits for them, and re-layouts: 86.5 us -> 0.08 us  [alpha_matrix(): matrices = jnp.take(alpha_table, type_of, axis=0)]
    select_n x41 -> x1, other arithmetic: 66 us -> 0.01 us  [alpha_matrix(): matrices = jnp.take(alpha_table, type_of, axis=0)]
    all_to_all x3 -> x0, local copies, waits for them, and re-layouts: 34.4 us -> none  [the longest x1 11.5 us: on_device(): lax.all_to_all(coeff_slots, 'col', split_axis=0, concat_axis=2, tiled=True)]
  transfers between devices with their start and end apart: 3 -> 5, of which waited for: 1 -> 3; matrix products, arithmetic and copies ran while one was open for 79% -> 12% of each run, Pallas kernels for 0% -> 4%
where the time goes in v1:
time: 435 us; the launch traced here: 434 us
  waiting for transfers between devices  191 us (44%)
  Pallas kernels  92.3 us (21%)
  blocking collectives  84.4 us (19%)
  local copies, waits for them, and re-layouts  29.2 us (7%)
  other arithmetic  23.2 us (5%)
  starting transfers between devices  14.1 us (3%)
    ppermute x3, waiting for transfers between devices, swapped(): return lax.ppermute(block, axis, route)  191 us
    all_to_all x2, blocking collectives, on_device(): got = lax.all_to_all(part, 'col', split_axis=0, concat_axis=0, tiled=True)  84.4 us
    pallas_call x1, Pallas kernels, beta_call(): pl.pallas_call(functools.partial(beta_kernel, groups, parts, block), out_...  65.2 us
    pallas_call x2, Pallas kernels, slots_call(): pl.pallas_call(kernel, out_shape=[out] * parts, grid=(width // chunk,), i...  27.1 us
    transpose x1, other arithmetic, alpha_matrix(): jnp.transpose(matrices, (0, 2, 1, 3)).reshape(count * block, count * block)  14.8 us
    gather x2, local copies, waits for them, and re-layouts, alpha_matrix(): matrices = jnp.take(alpha_table, type_of, axis=0)  11.7 us
  transfers between devices with their start and end apart: 5, of which 3 were waited for; matrix products, arithmetic and copies ran while one was open for 12% of the time, Pallas kernels for 4%

profile of v1, /device:TPU:0, one launch (start us, length us, event | category | flops | bytes accessed | tf_op | source)
XLA Modules:
  0.0 434.3 jit_solution(15170761554647849801)
XLA Ops:
  0.0 0.9 reduce-window.9
  0.9 1.2 bitcast_subtract_fusion.starts
  2.1 8.6 %coeff_slots.1 = (f32[8,64,1536]{2,1,0:T(8,128)}, f32[8,64,1536]{2,1,0:T(8,128)}, f32[8,64,1536]{2,1,0:T(8,128)}) custom-call(s32[8]{0:T(128)} %bitcast_subtract_fusion.starts, f32[1536,1024]{1,0:T(8,128)} %coeffs.3), custom_call_target="tpu_custom_call" | custom-call | tf_op jit(solution)/shard_map/coeff_slots/pallas_call | solution.py:83
  10.7 43.4 %all_to_all.20.rest_0_ = f32[8,64,1536]{2,1,0:T(8,128)} all-to-all(f32[8,64,1536]{2,1,0:T(8,128)} %get-tuple-element.8), channel_id=1, replica_groups=mesh['cls'=4,'col'=8] {'col'}, dimensions={0} | all-to-all | bytes 6291456 | tf_op jit(solution)/shard_map/all_to_all | solution.py:232
  54.1 41.0 %all_to_all.21.rest_1_ = f32[8,64,1536]{2,1,0:T(8,128)} all-to-all(f32[8,64,1536]{2,1,0:T(8,128)S(1)} %copy-done.2), channel_id=1, replica_groups=mesh['cls'=4,'col'=8] {'col'}, dimensions={0} | all-to-all | bytes 6291456 | tf_op jit(solution)/shard_map/all_to_all | solution.py:232
  95.1 4.6 %all-to-all-start.2 = ((f32[8,64,1536]{2,1,0:T(8,128)}), f32[8,64,1536]{2,1,0:T(8,128)}, u32[]{:S(2)}, u32[]{:S(2)}) async-start(f32[8,64,1536]{2,1,0:T(8,128)} %get-tuple-element.10), calls=%async_computation.2 | async-start | bytes 6291456 | tf_op jit(solution)/shard_map/all_to_all | solution.py:232
  99.7 0.1 select_reduce_fusion
  99.9 0.1 reshape.69
  100.0 3.9 gather_fusion
  103.9 7.8 %gather.7 = f32[16,16,64,64]{3,2,1,0:T(8,128)} reshape(f32[256,4096]{1,0:T(8,128)} %gather_fusion) | data formatting | bytes 8388608 | tf_op jit(solution)/shard_map/jit(_take)/gather | solution.py:187
  111.7 0.1 fusion.4
  111.8 14.8 %fusion.1 = f32[16,64,16,64]{3,2,1,0:T(8,128)} fusion(f32[16,16,64,64]{3,2,1,0:T(8,128)} %gather.7, pred[16,16]{1,0:T(8,128)(4,1)S(1)} %compare_and_fusion, pred[16,16]{1,0:T(8,128)(4,1)S(1)} %fusion.4), kind=kLoop, calls=%fused_computation.3 | loop fusion | flops 2097152 | bytes 8389120 | tf_op jit(solution)/shard_map/transpose | solution.py:190
  126.6 7.6 %reshape.65 = f32[1024,1024]{1,0:T(8,128)} reshape(f32[16,64,16,64]{3,2,1,0:T(8,128)} %fusion.1) | data formatting | bytes 8388608 | tf_op jit(solution)/shard_map/reshape | solution.py:190
  134.2 5.1 %fusion.2 = (bf16[1024,1024]{1,0:T(8,128)(2,1)}, bf16[1024,1024]{1,0:T(8,128)(2,1)}) fusion(f32[1024,1024]{1,0:T(8,128)} %reshape.65), kind=kLoop, calls=%fused_computation.6 | loop fusion | flops 4194304 | bytes 8388608 | tf_op jit(solution)/shard_map/convert_element_type | solution.py:27
  139.3 18.5 %alpha_slots.1 = f32[8,192,1536]{2,1,0:T(8,128)} custom-call(s32[8]{0:T(128)} %bitcast_subtract_fusion.starts, f32[1536,1024]{1,0:T(8,128)} %coeffs.3, bf16[1024,1024]{1,0:T(8,128)(2,1)} %get-tuple-element.12.high_ref, bf16[1024,1024]{1,0:T(8,128)(2,1)} %get-tuple-element.11.low_ref), custom_call_target="tpu_custom_call" | custom-call | tf_op jit(solution)/shard_map/alpha_slots/pallas_call | solution.py:83
  157.8 5.2 %all-to-all-start.3 = ((f32[8,192,1536]{2,1,0:T(8,128)}), f32[8,192,1536]{2,1,0:T(8,128)}, u32[]{:S(2)}, u32[]{:S(2)}) async-start(f32[8,192,1536]{2,1,0:T(8,128)} %alpha_slots.1), calls=%async_computation.3 | async-start | bytes 18874368 | tf_op jit(solution)/shard_map/all_to_all | solution.py:239
  163.0 2.2 collective-permute-start.2
  165.4 1.9 collective-permute-start
  167.3 0.6 dynamic_slice.3.keep
  167.9 0.1 copy.14
  168.0 0.7 reshape.61.entries
  168.7 0.1 copy.15
  168.8 0.7 reshape.62.types
  169.5 2.3 reshape.66
  171.8 1.9 copy.17
  173.7 0.4 reduce-precision_convert_fusion.1
  174.1 0.6 pad_maximum_fusion
  174.7 3.4 fusion.5
  178.1 56.4 %collective-permute-done.2.rest_5_ = f32[8,64,1536]{2,1,0:T(8,128)} collective-permute-done((f32[8,64,1536]{2,1,0:T(8,128)}, f32[8,64,1536]{2,1,0:T(8,128)}, u32[]{:S(2)}, u32[]{:S(2)}) %collective-permute-start.2) | collective-permute-done | bytes 3145760 | tf_op jit(solution)/shard_map/ppermute | solution.py:22
  234.5 67.4 %collective-permute-done.1.rest_4_ = f32[8,64,1536]{2,1,0:T(8,128)} collective-permute-done((f32[8,64,1536]{2,1,0:T(8,128)}, f32[8,64,1536]{2,1,0:T(8,128)}, u32[]{:S(2)}, u32[]{:S(2)}) %collective-permute-start.1) | collective-permute-done | bytes 3145760 | tf_op jit(solution)/shard_map/ppermute | solution.py:22
  301.9 67.1 %collective-permute-done.rest_3_ = f32[8,64,1536]{2,1,0:T(8,128)} collective-permute-done((f32[8,64,1536]{2,1,0:T(8,128)}, f32[8,64,1536]{2,1,0:T(8,128)}, u32[]{:S(2)}, u32[]{:S(2)}) %collective-permute-start) | collective-permute-done | bytes 3145760 | tf_op jit(solution)/shard_map/ppermute | solution.py:22
  369.0 65.2 %beta_sum.1 = f32[192,12288]{1,0:T(8,128)} custom-call(s32[1]{0:T(128)} %dynamic_slice.3.keep, s32[2304]{0:T(1024)} %reshape.61.entries, s32[2304]{0:T(1024)} %reshape.62.types, f32[8,64,1536]{2,1,0:T(8,128)} %all_to_all.20.rest_0_, f32[8,64,1536]{2,1,0:T(8,128)} %all_to_all.21.rest_1_, f32[8,64,1536]{2,1,0:T(8,128)} %all-to-all-done.2.rest_2_, ...), custom_call_target="tpu_custom_call" | custom-call | tf_op jit(solution)/shard_map/beta_sum/pallas_call | solution.py:166
  (24 shorter events, 0.1 us)
Async XLA Ops:
  0.0 100.0 %copy-start = (f32[64,4096]{1,0:T(8,128)S(1)}, f32[64,4096]{1,0:T(8,128)}, u32[]{:S(2)}) copy-start(f32[64,4096]{1,0:T(8,128)} %param.9) | copy-start | bytes 3145732
  10.7 43.4 %copy-start.2 = (f32[8,64,1536]{2,1,0:T(8,128)S(1)}, f32[8,64,1536]{2,1,0:T(8,128)}, u32[]{:S(2)}) copy-start(f32[8,64,1536]{2,1,0:T(8,128)} %get-tuple-element.9) | copy-start | bytes 9437188
  95.1 4.6 %copy-start.4 = (s32[16,16]{1,0:T(8,128)S(1)}, s32[16,16]{1,0:T(8,128)}, u32[]{:S(2)}) copy-start(s32[16,16]{1,0:T(8,128)} %param.10) | copy-start | bytes 3076
  95.1 4.6 %copy-start.7 = (s32[16,16]{1,0:T(8,128)S(1)}, s32[16,16]{1,0:T(8,128)}, u32[]{:S(2)}) copy-start(s32[16,16]{1,0:T(8,128)} %param.11) | copy-start | bytes 3076
  95.1 62.7 %all-to-all-start.2 = ((f32[8,64,1536]{2,1,0:T(8,128)}), f32[8,64,1536]{2,1,0:T(8,128)}, u32[]{:S(2)}, u32[]{:S(2)}) async-start(f32[8,64,1536]{2,1,0:T(8,128)} %get-tuple-element.10), calls=%async_computation.2 | async-start | bytes 6291456 | tf_op jit(solution)/shard_map/all_to_all | solution.py:232
  157.8 9.5 %copy-start.8 = (s32[8]{0:T(128)S(1)}, s32[8]{0:T(128)}, u32[]{:S(2)}) copy-start(s32[8]{0:T(128)} %param.15) | copy-start | bytes 100
  157.8 10.1 %copy-start.5 = (s32[192,12]{0,1:T(8,128)S(1)}, s32[192,12]{0,1:T(8,128)}, u32[]{:S(2)}) copy-start(s32[192,12]{0,1:T(8,128)} %param.13) | copy-start | bytes 27652
  157.8 10.9 %copy-start.6 = (s32[192,12]{0,1:T(8,128)S(1)}, s32[192,12]{0,1:T(8,128)}, u32[]{:S(2)}) copy-start(s32[192,12]{0,1:T(8,128)} %param.14) | copy-start | bytes 27652
  157.8 11.7 %copy-start.3 = (f32[64,4096]{1,0:T(8,128)S(1)}, f32[64,4096]{1,0:T(8,128)}, u32[]{:S(2)}) copy-start(f32[64,4096]{1,0:T(8,128)} %param.12) | copy-start | bytes 3145732
  157.8 211.2 %all-to-all-start.3 = ((f32[8,192,1536]{2,1,0:T(8,128)}), f32[8,192,1536]{2,1,0:T(8,128)}, u32[]{:S(2)}, u32[]{:S(2)}) async-start(f32[8,192,1536]{2,1,0:T(8,128)} %alpha_slots.1), calls=%async_computation.3 | async-start | bytes 18874368 | tf_op jit(solution)/shard_map/all_to_all | solution.py:239
  163.0 71.4 %collective-permute-start.2 = (f32[8,64,1536]{2,1,0:T(8,128)}, f32[8,64,1536]{2,1,0:T(8,128)}, u32[]{:S(2)}, u32[]{:S(2)}) collective-permute-start(f32[8,64,1536]{2,1,0:T(8,128)} %all-to-all-done.2.rest_2_), channel_id=1, source_target_pairs={{0,8},{8,0},{16,24},{24,16},{1,9},{9,1},{17,25},{25,17},{2,10},{10... | collective-permute-start | bytes 9437192 | tf_op jit(solution)/shard_map/ppermute | solution.py:22
  165.3 136.6 %collective-permute-start.1 = (f32[8,64,1536]{2,1,0:T(8,128)}, f32[8,64,1536]{2,1,0:T(8,128)}, u32[]{:S(2)}, u32[]{:S(2)}) collective-permute-start(f32[8,64,1536]{2,1,0:T(8,128)} %all_to_all.21.rest_1_), channel_id=1, source_target_pairs={{0,8},{8,0},{16,24},{24,16},{1,9},{9,1},{17,25},{25,17},{2,10},{10... | collective-permute-start | bytes 9437192 | tf_op jit(solution)/shard_map/ppermute | solution.py:22
  165.4 203.6 %collective-permute-start = (f32[8,64,1536]{2,1,0:T(8,128)}, f32[8,64,1536]{2,1,0:T(8,128)}, u32[]{:S(2)}, u32[]{:S(2)}) collective-permute-start(f32[8,64,1536]{2,1,0:T(8,128)} %all_to_all.20.rest_0_), channel_id=1, source_target_pairs={{0,8},{8,0},{16,24},{24,16},{1,9},{9,1},{17,25},{25,17},{2,10},{10... | collective-permute-start | bytes 9437192 | tf_op jit(solution)/shard_map/ppermute | solution.py:22
  369.0 65.2 %copy-start.1 = (f32[64,4096]{1,0:T(8,128)S(1)}, f32[64,4096]{1,0:T(8,128)}, u32[]{:S(2)}) copy-start(f32[64,4096]{1,0:T(8,128)} %param.9) | copy-start | bytes 3145732

commit v2 on v1

--- a/solution.py
+++ b/solution.py
@@ -10,16 +10,6 @@
 ROW_PARTS = 3
 TILE = 8
 VMEM_BYTES = 56 * 1024 * 1024
-
-
-def swapped(block, axis, apart):
-    count = lax.axis_size(axis)
-    route = []
-    for low in range(count):
-        high = low | 1 << apart
-        if high != low and high < count:
-            route += [(low, high), (high, low)]
-    return lax.ppermute(block, axis, route)
 
 
 def split_outside(x):
@@ -60,22 +50,38 @@
     write_slots(starts, tall, out_refs)
 
 
-def alpha_kernel(starts, coeffs, high_ref, low_ref, out_ref, tall):
+def alpha_kernel(block, starts, types, coeffs, left, right, out_ref, tall, a_high, a_low):
     rows = coeffs.shape[1]
+    count = rows // block
+
+    @pl.when(pl.program_id(0) == 0)
+    def _():
+        def fill(at, carry):
+            place = pl.ds(pl.multiple_of(at * block, block), block)
+            for other in range(0, count, 2):
+                first = types[at * count + other]
+                second = types[at * count + other + 1]
+                both = left[first] + right[second]
+                a_high[place, other * block : (other + 2) * block] = both[:block]
+                a_low[place, other * block : (other + 2) * block] = both[block:]
+            return carry
+
+        lax.fori_loop(0, count, fill, 0)
+
     c_high, c_low = split_inside(coeffs[...])
     dot = functools.partial(
         lax.dot_general,
         dimension_numbers=(((1,), (1,)), ((), ())),
         preferred_element_type=jnp.float32,
     )
-    tall[:rows, :] = (dot(low_ref[...], c_high) + dot(high_ref[...], c_low)) + dot(
-        high_ref[...], c_high
+    tall[:rows, :] = (dot(a_low[...], c_high) + dot(a_high[...], c_low)) + dot(
+        a_high[...], c_high
     )
     tall[rows:, :] = jnp.zeros((tall.shape[0] - rows, tall.shape[1]), jnp.float32)
     write_slots(starts, tall, [out_ref])
 
 
-def slots_call(kernel, coeffs_t, starts, matrices, groups, capacity, parts, name):
+def slots_call(kernel, coeffs_t, scalars, tables, scratch, groups, capacity, parts, name):
     width, rows = coeffs_t.shape
     chunk = column_chunk(width)
     piece = capacity // parts
@@ -84,16 +90,14 @@
         kernel,
         out_shape=[out] * parts,
         grid=(width // chunk,),
-        in_specs=[
-            pl.BlockSpec(memory_space=pltpu.SMEM),
-            pl.BlockSpec((chunk, rows), lambda i: (i, 0)),
-        ]
-        + [pl.BlockSpec(m.shape, lambda i: (0, 0)) for m in matrices],
+        in_specs=[pl.BlockSpec(memory_space=pltpu.SMEM)] * len(scalars)
+        + [pl.BlockSpec((chunk, rows), lambda i: (i, 0))]
+        + [pl.BlockSpec(table.shape, lambda i: (0, 0, 0)) for table in tables],
         out_specs=[pl.BlockSpec((groups, piece, chunk), lambda i: (0, 0, i))] * parts,
-        scratch_shapes=[pltpu.VMEM((rows + capacity + TILE, chunk), jnp.float32)],
+        scratch_shapes=[pltpu.VMEM((rows + capacity + TILE, chunk), jnp.float32), *scratch],
         compiler_params=pltpu.CompilerParams(vmem_limit_bytes=VMEM_BYTES),
         name=name,
-    )(starts, coeffs_t, *matrices)
+    )(*scalars, coeffs_t, *tables)
 
 
 def beta_kernel(steps, parts, block, keep, entries, types, *rest):
@@ -180,23 +184,141 @@
     )(keep, entries, types, *own, *partner, alpha, left, right)
 
 
-def alpha_matrix(alpha_table, alpha_blocks, alpha_types, block):
+def exchange_kernel(groups, parts, *refs):
+    own, alpha = refs[:parts], refs[parts]
+    refs = refs[parts + 1 :]
+    own_in, partner_in, alpha_in = refs[:parts], refs[parts : 2 * parts], refs[2 * parts]
+    own_send, own_recv, far_send, far_recv, alpha_send, alpha_recv, local = refs[2 * parts + 1 :]
+    cls, me = lax.axis_index("cls"), lax.axis_index("col")
+    other = cls ^ 1
+
+    barrier = pltpu.get_barrier_semaphore()
+    for apart in range(1, groups):
+        pl.semaphore_signal(
+            barrier, inc=1, device_id=(cls, me ^ apart), device_id_type=pl.DeviceIdType.MESH
+        )
+    pl.semaphore_signal(
+        barrier, inc=1, device_id=(other, me), device_id_type=pl.DeviceIdType.MESH
+    )
+    pl.semaphore_wait(barrier, groups)
+
+    def near(source, target, apart, send, recv):
+        return pltpu.make_async_remote_copy(
+            src_ref=source.at[me ^ apart],
+            dst_ref=target.at[me],
+            send_sem=send,
+            recv_sem=recv,
+            device_id=(cls, me ^ apart),
+            device_id_type=pl.DeviceIdType.MESH,
+        )
+
+    def far(part, apart):
+        source = own[part] if apart == 0 else own_in[part]
+        return pltpu.make_async_remote_copy(
+            src_ref=source.at[me ^ apart],
+            dst_ref=partner_in[part].at[me ^ apart],
+            send_sem=far_send.at[part, apart],
+            recv_sem=far_recv.at[part, apart],
+            device_id=(other, me),
+            device_id_type=pl.DeviceIdType.MESH,
+        )
+
+    aparts = range(1, groups)
+    own_copies = [
+        [near(own[p], own_in[p], x, own_send.at[p, x], own_recv.at[p, x]) for x in aparts]
+        for p in range(parts)
+    ]
+    alpha_copies = [near(alpha, alpha_in, x, alpha_send.at[x], alpha_recv.at[x]) for x in aparts]
+    far_copies = [[far(p, x) for x in range(groups)] for p in range(parts)]
+    local_copies = [
+        pltpu.make_async_copy(own[p].at[me], own_in[p].at[me], local.at[p]) for p in range(parts)
+    ] + [pltpu.make_async_copy(alpha.at[me], alpha_in.at[me], local.at[parts])]
+    waves = own_copies + [alpha_copies]
+
+    for part in range(parts):
+        far_copies[part][0].start()
+    for copy in waves[0] + waves[1]:
+        copy.start()
+    for copy in local_copies:
+        copy.start()
+    for part in range(parts):
+        for at, copy in enumerate(own_copies[part]):
+            copy.wait_recv()
+            far_copies[part][at + 1].start()
+        if part + 2 < len(waves):
+            for copy in waves[part + 2]:
+                copy.start()
+    for copy in alpha_copies:
+        copy.wait_recv()
+    for copies in far_copies:
+        for copy in copies:
+            copy.wait_recv()
+    for copy in local_copies:
+        copy.wait()
+    for copies in waves + far_copies:
+        for copy in copies:
+            copy.wait_send()
+
+
+def exchange_call(own, alpha):
+    groups = alpha.shape[0]
+    parts = len(own)
+    shape = lambda x: jax.ShapeDtypeStruct(x.shape, x.dtype)
+    outs = [shape(x) for x in own] * 2 + [shape(alpha)]
+    dma = pltpu.SemaphoreType.DMA
+    got = pl.pallas_call(
+        functools.partial(exchange_kernel, groups, parts),
+        out_shape=outs,
+        in_specs=[pl.BlockSpec(memory_space=pl.ANY)] * (parts + 1),
+        out_specs=[pl.BlockSpec(memory_space=pl.ANY)] * len(outs),
+        scratch_shapes=[dma((parts, groups))] * 4 + [dma((groups,))] * 2 + [dma((parts + 1,))],
+        compiler_params=pltpu.CompilerParams(
+            collective_id=0, has_side_effects=True, vmem_limit_bytes=VMEM_BYTES
+        ),
+        name="exchange",
+    )(*own, alpha)
+    return got[:parts], got[parts : 2 * parts], got[2 * parts]
+
+
+def alpha_entries(alpha_blocks, alpha_types, missing):
     count = alpha_blocks.shape[0]
     hit = alpha_blocks[:, :, None] == jnp.arange(count, dtype=jnp.int32)[None, None, :]
     type_of = jnp.sum(jnp.where(hit, alpha_types[:, :, None], 0), 1)
-    matrices = jnp.take(alpha_table, type_of, axis=0)
-    matrices = jnp.where(jnp.any(hit, 1)[:, :, None], matrices, jnp.float32(0.0))
-    matrices = matrices.reshape(count, count, block, block)
-    return jnp.transpose(matrices, (0, 2, 1, 3)).reshape(count * block, count * block)
-
-
-def beta_weights(beta_table, block):
-    tables = jnp.transpose(beta_table.reshape(-1, block, block), (0, 2, 1))
+    return jnp.where(jnp.any(hit, 1), type_of, missing).reshape(-1).astype(jnp.int32)
+
+
+def weights(tables):
+    block = tables.shape[2]
     both = jnp.concatenate(split_outside(tables), 1)
     return (
         jnp.pad(both, ((0, 0), (0, 0), (0, block))),
         jnp.pad(both, ((0, 0), (0, 0), (block, 0))),
     )
+
+
+def alpha_weights(alpha_table, block):
+    tables = alpha_table.reshape(-1, block, block)
+    return weights(jnp.pad(tables, ((0, 1), (0, 0), (0, 0))))
+
+
+def beta_weights(beta_table, block):
+    return weights(jnp.transpose(beta_table.reshape(-1, block, block), (0, 2, 1)))
+
+
+def alpha_call(coeffs_t, starts, alpha_table, alpha_blocks, alpha_types, groups, capacity, block):
+    rows = coeffs_t.shape[1]
+    types = alpha_entries(alpha_blocks, alpha_types, alpha_table.shape[0])
+    return slots_call(
+        functools.partial(alpha_kernel, block),
+        coeffs_t,
+        (starts, types),
+        alpha_weights(alpha_table, block),
+        [pltpu.VMEM((rows, rows), jnp.bfloat16)] * 2,
+        groups,
+        capacity,
+        1,
+        "alpha_slots",
+    )[0]
 
 
 def even_wide(x, block):
@@ -225,18 +347,12 @@
     keep = lax.dynamic_slice(row_counts, (lax.axis_index("col"),), (1,))
 
     coeff_slots = slots_call(
-        coeff_kernel, coeffs_t, starts, (), groups, capacity, ROW_PARTS, "coeff_slots"
-    )
-    own, partner = [], []
-    for part in coeff_slots:
-        got = lax.all_to_all(part, "col", split_axis=0, concat_axis=0, tiled=True)
-        own.append(got)
-        partner.append(swapped(got, "cls", 0))
-    matrix = split_outside(alpha_matrix(alpha_table, alpha_blocks, alpha_types, block))
-    (alpha_slots,) = slots_call(
-        alpha_kernel, coeffs_t, starts, matrix, groups, capacity, 1, "alpha_slots"
-    )
-    alpha = lax.all_to_all(alpha_slots, "col", split_axis=0, concat_axis=0, tiled=True)
+        coeff_kernel, coeffs_t, (starts,), (), (), groups, capacity, ROW_PARTS, "coeff_slots"
+    )
+    alpha_slots = alpha_call(
+        coeffs_t, starts, alpha_table, alpha_blocks, alpha_types, groups, capacity, block
+    )
+    own, partner, alpha = exchange_call(coeff_slots, alpha_slots)
     left, right = beta_weights(beta_table, block)
     wide = lambda x: even_wide(x, block)
     return beta_call(

time: 435 us -> 323 us (0.74)
  Pallas kernels: 92.3 us -> 304 us
  waiting for transfers between devices: 191 us -> 0 us
  blocking collectives: 84.4 us -> 0 us
  other arithmetic: 23.2 us -> 3.29 us
  starting transfers between devices: 14.1 us -> 0 us
  local copies, waits for them, and re-layouts: 29.2 us -> 15.5 us
    pallas_call x0 -> x1, Pallas kernels: none -> 210 us  [exchange_call(): pl.pallas_call(functools.partial(exchange_kernel, groups, parts), out_sha...]
    ppermute x3 -> x0, waiting for transfers between devices: 191 us -> none  [swapped(): return lax.ppermute(block, axis, route)]
    all_to_all x2 -> x0, blocking collectives: 84.4 us -> none  [on_device(): got = lax.all_to_all(part, 'col', split_axis=0, concat_axis=0, tiled=True)]
    transpose x1 -> x0, other arithmetic: 14.8 us -> none  [alpha_matrix(): jnp.transpose(matrices, (0, 2, 1, 3)).reshape(count * block, count * block)]
    gather x2 -> x0, local copies, waits for them, and re-layouts: 11.7 us -> none  [alpha_matrix(): matrices = jnp.take(alpha_table, type_of, axis=0)]
    all_to_all x2 -> x0, starting transfers between devices: 9.79 us -> none  [the longest x1 5.19 us: on_device(): lax.all_to_all(alpha_slots, 'col', split_axis=0, concat_axis=0, tiled=True)]
    reshape x3, local copies, waits for them, and re-layouts: 11.8 us -> 6.25 us  [the longest x2 4.25 us: beta_weights(): beta_table.reshape(-1, block, block)]
  transfers between devices with their start and end apart: 5 -> 0, of which waited for: 3 -> 0; matrix products, arithmetic and copies ran while one was open for 12% -> 0% of each run, Pallas kernels for 4% -> 0%
where the time goes in v2:
time: 323 us
  Pallas kernels  304 us (94%)
  local copies, waits for them, and re-layouts  15.5 us (5%)
  other arithmetic  3.29 us (1%)
    pallas_call x1, Pallas kernels, exchange_call(): pl.pallas_call(functools.partial(exchange_kernel, groups, parts), out_sha...  210 us
    pallas_call x1, Pallas kernels, beta_call(): pl.pallas_call(functools.partial(beta_kernel, groups, parts, block), out_...  65.1 us
    pallas_call x2, Pallas kernels, slots_call(): pl.pallas_call(kernel, out_shape=[out] * parts, grid=(width // chunk,), i...  28.5 us

profile of v2, /device:TPU:0, one launch (start us, length us, event | category | flops | bytes accessed | tf_op | source)
XLA Modules:
  0.0 322.7 jit_solution(6470601851732838808)
XLA Ops:
  0.0 2.0 reshape.49
  2.0 0.6 reduce-precision_convert_fusion
  2.6 0.6 pad_maximum_fusion
  3.2 0.0 copy-start.5
  3.2 0.0 copy-start.1
  3.2 0.0 copy-start.4
  3.2 2.9 fusion.3
  6.2 0.0 copy-done.5
  6.2 0.2 reduce-window.9
  6.3 0.5 bitcast_subtract_fusion.starts
  6.9 0.0 copy-done.1
  6.9 0.0 copy-done.4
  6.9 0.1 select_reduce_fusion
  7.0 0.1 fusion.2
  7.2 0.6 select_n.18.types
  7.8 20.0 %alpha_slots.1.refs_3_ = f32[8,192,1536]{2,1,0:T(8,128)} custom-call(s32[8]{0:T(128)} %bitcast_subtract_fusion.starts, s32[256]{0:T(256)} %select_n.18.types, f32[1536,1024]{1,0:T(8,128)} %coeffs.3, bf16[65,128,128]{2,1,0:T(8,128)(2,1)} %get-tuple-element.26.left, bf16[65,128,128]{2,1,0:T(8,128)(2,1)} %get-tuple-element.25.right), custom_call_target="tpu_custom_call" | custom-call | tf_op jit(solution)/shard_map/alpha_slots/pallas_call | solution.py:89
  27.8 8.5 %coeff_slots.1 = (f32[8,64,1536]{2,1,0:T(8,128)}, f32[8,64,1536]{2,1,0:T(8,128)}, f32[8,64,1536]{2,1,0:T(8,128)}) custom-call(s32[8]{0:T(128)} %bitcast_subtract_fusion.starts, f32[1536,1024]{1,0:T(8,128)} %coeffs.3), custom_call_target="tpu_custom_call" | custom-call | tf_op jit(solution)/shard_map/coeff_slots/pallas_call | solution.py:89
  36.3 210.1 %exchange.1 = (f32[8,64,1536]{2,1,0:T(8,128)}, f32[8,64,1536]{2,1,0:T(8,128)}, f32[8,64,1536]{2,1,0:T(8,128)}, f32[8,64,1536]{2,1,0:T(8,128)}, f32[8,64,1536]{2,...) custom-call(f32[8,64,1536]{2,1,0:T(8,128)} %get-tuple-element.15.refs_0_, ...), custom_call_target="tpu_custom_call" | custom-call | tf_op jit(solution)/shard_map/exchange/pallas_call | solution.py:269
  246.5 0.7 dynamic_slice.3.keep
  247.1 0.0 copy-done
  247.1 2.2 reshape.50
  249.3 2.1 copy.14
  251.4 0.6 reduce-precision_convert_fusion.1
  252.0 0.6 pad_maximum_fusion.1
  252.6 0.0 copy-start.2
  252.6 0.0 copy-start.3
  252.6 3.4 %fusion.4 = (bf16[64,128,128]{2,1,0:T(8,128)(2,1)}, bf16[64,128,128]{2,1,0:T(8,128)(2,1)}) fusion(bf16[64,128,64]{2,1,0:T(8,128)(2,1)S(1)} %pad_maximum_fusion.1), kind=kLoop, calls=%fused_computation.14 | loop fusion | bytes 5242880 | tf_op jit(solution)/shard_map/jit(_pad)/pad | solution.py:295
  256.0 0.1 copy.12
  256.1 0.7 reshape.45.entries
  256.8 0.1 copy.13
  256.9 0.7 reshape.46.types
  257.6 65.1 %beta_sum.1 = f32[192,12288]{1,0:T(8,128)} custom-call(s32[1]{0:T(128)} %dynamic_slice.3.keep, s32[2304]{0:T(1024)} %reshape.45.entries, s32[2304]{0:T(1024)} %reshape.46.types, f32[8,64,1536]{2,1,0:T(8,128)} %get-tuple-element.18.rest_0_, f32[8,64,1536]{2,1,0:T(8,128)} %get-tuple-element.19.rest_1_, f32[8,64,1536]{2,1,0:T(8,128)} %get-tuple-element.20.rest_2_, ...), custom_call_target="tpu_custom_call" | custom-call | tf_op jit(solution)/shard_map/beta_sum/pallas_call | solution.py:170
  (4 shorter events, 0.0 us)
Async XLA Ops:
  3.2 3.0 copy-start.5
  3.2 3.7 %copy-start.1 = (s32[16,16]{1,0:T(8,128)S(1)}, s32[16,16]{1,0:T(8,128)}, u32[]{:S(2)}) copy-start(s32[16,16]{1,0:T(8,128)} %param.10) | copy-start | bytes 3076
  3.2 3.7 %copy-start.4 = (s32[16,16]{1,0:T(8,128)S(1)}, s32[16,16]{1,0:T(8,128)}, u32[]{:S(2)}) copy-start(s32[16,16]{1,0:T(8,128)} %param.11) | copy-start | bytes 3076
  36.3 210.8 %copy-start = (f32[64,4096]{1,0:T(8,128)S(1)}, f32[64,4096]{1,0:T(8,128)}, u32[]{:S(2)}) copy-start(f32[64,4096]{1,0:T(8,128)} %param.12) | copy-start | bytes 3145732
  252.6 3.4 %copy-start.2 = (s32[192,12]{0,1:T(8,128)S(1)}, s32[192,12]{0,1:T(8,128)}, u32[]{:S(2)}) copy-start(s32[192,12]{0,1:T(8,128)} %param.13) | copy-start | bytes 27652
  252.6 4.2 %copy-start.3 = (s32[192,12]{0,1:T(8,128)S(1)}, s32[192,12]{0,1:T(8,128)}, u32[]{:S(2)}) copy-start(s32[192,12]{0,1:T(8,128)} %param.14) | copy-start | bytes 27652

commit v3 on v2

--- a/solution.py
+++ b/solution.py
@@ -50,54 +50,76 @@
     write_slots(starts, tall, out_refs)
 
 
-def alpha_kernel(block, starts, types, coeffs, left, right, out_ref, tall, a_high, a_low):
-    rows = coeffs.shape[1]
+def alpha_rows_kernel(block, starts, types, left, right, high_ref, low_ref, tall):
+    rows = tall.shape[1]
     count = rows // block
-
-    @pl.when(pl.program_id(0) == 0)
-    def _():
-        def fill(at, carry):
-            place = pl.ds(pl.multiple_of(at * block, block), block)
-            for other in range(0, count, 2):
-                first = types[at * count + other]
-                second = types[at * count + other + 1]
-                both = left[first] + right[second]
-                a_high[place, other * block : (other + 2) * block] = both[:block]
-                a_low[place, other * block : (other + 2) * block] = both[block:]
-            return carry
-
-        lax.fori_loop(0, count, fill, 0)
-
-    c_high, c_low = split_inside(coeffs[...])
+    groups, capacity = high_ref.shape[:2]
+
+    def fill(at, carry):
+        place = pl.ds(pl.multiple_of(at * block, block), block)
+        for other in range(0, count, 2):
+            first = types[at * count + other]
+            second = types[at * count + other + 1]
+            tall[place, other * block : (other + 2) * block] = left[first] + right[second]
+        return carry
+
+    lax.fori_loop(0, count, fill, 0)
+    tall[rows:, :] = jnp.zeros((tall.shape[0] - rows, rows), jnp.float32)
+    for slot in range(groups):
+        shift = lax.rem(starts[slot], TILE)
+        span = capacity + TILE
+        place = pl.ds(pl.multiple_of(starts[slot] - shift, TILE), span)
+        moved = pltpu.roll(tall[place, :], lax.rem(span - shift, span), 0)
+        high_ref[slot], low_ref[slot] = split_inside(moved[:capacity])
+
+
+def alpha_rows_call(starts, types, left, right, rows, groups, capacity, block):
+    out = jax.ShapeDtypeStruct((groups, capacity, rows), jnp.bfloat16)
+    return pl.pallas_call(
+        functools.partial(alpha_rows_kernel, block),
+        out_shape=[out] * 2,
+        in_specs=[pl.BlockSpec(memory_space=pltpu.SMEM)] * 2
+        + [pl.BlockSpec(memory_space=pltpu.VMEM)] * 2,
+        out_specs=[pl.BlockSpec(memory_space=pltpu.VMEM)] * 2,
+        scratch_shapes=[pltpu.VMEM((rows + capacity + TILE, rows), jnp.float32)],
+        compiler_params=pltpu.CompilerParams(vmem_limit_bytes=VMEM_BYTES),
+        name="alpha_rows",
+    )(starts, types, left, right)
+
+
+def alpha_product(chunk, coeffs, a_high, a_low, out):
     dot = functools.partial(
         lax.dot_general,
         dimension_numbers=(((1,), (1,)), ((), ())),
         preferred_element_type=jnp.float32,
     )
-    tall[:rows, :] = (dot(a_low[...], c_high) + dot(a_high[...], c_low)) + dot(
-        a_high[...], c_high
-    )
-    tall[rows:, :] = jnp.zeros((tall.shape[0] - rows, tall.shape[1]), jnp.float32)
-    write_slots(starts, tall, [out_ref])
-
-
-def slots_call(kernel, coeffs_t, scalars, tables, scratch, groups, capacity, parts, name):
+    for first in range(0, coeffs.shape[0], chunk):
+        c_high, c_low = split_inside(coeffs[first : first + chunk, :])
+        for slot in range(out.shape[0]):
+            total = (dot(a_low[slot], c_high) + dot(a_high[slot], c_low)) + dot(
+                a_high[slot], c_high
+            )
+            out[slot, :, first : first + chunk] = total
+
+
+def slots_call(coeffs_t, starts, groups, capacity, parts):
     width, rows = coeffs_t.shape
     chunk = column_chunk(width)
     piece = capacity // parts
     out = jax.ShapeDtypeStruct((groups, piece, width), jnp.float32)
     return pl.pallas_call(
-        kernel,
+        coeff_kernel,
         out_shape=[out] * parts,
         grid=(width // chunk,),
-        in_specs=[pl.BlockSpec(memory_space=pltpu.SMEM)] * len(scalars)
-        + [pl.BlockSpec((chunk, rows), lambda i: (i, 0))]
-        + [pl.BlockSpec(table.shape, lambda i: (0, 0, 0)) for table in tables],
+        in_specs=[
+            pl.BlockSpec(memory_space=pltpu.SMEM),
+            pl.BlockSpec((chunk, rows), lambda i: (i, 0)),
+        ],
         out_specs=[pl.BlockSpec((groups, piece, chunk), lambda i: (0, 0, i))] * parts,
-        scratch_shapes=[pltpu.VMEM((rows + capacity + TILE, chunk), jnp.float32), *scratch],
+        scratch_shapes=[pltpu.VMEM((rows + capacity + TILE, chunk), jnp.float32)],
         compiler_params=pltpu.CompilerParams(vmem_limit_bytes=VMEM_BYTES),
-        name=name,
-    )(*scalars, coeffs_t, *tables)
+        name="coeff_slots",
+    )(starts, coeffs_t)
 
 
 def beta_kernel(steps, parts, block, keep, entries, types, *rest):
@@ -146,15 +168,20 @@
         row = lax.broadcasted_iota(jnp.int32, (out.shape[0], 2 * block), 0)
         kept = row < keep[0]
 
-        def pair(at, carry):
-            m = first + 2 * at
-            tall = jnp.concatenate([one(m), one(m + 1)], 0)
-            lanes = pl.ds(pl.multiple_of(at * (2 * block), 2 * block), 2 * block)
-            total = tall.T + alpha[0, :, lanes]
-            out[:, lanes] = jnp.where(kept, total, jnp.float32(0.0))
+        pairs = width // (2 * block)
+        together = 4 if pairs % 4 == 0 else 1
+
+        def some_pairs(turn, carry):
+            for nth in range(together):
+                at = turn * together + nth
+                m = first + 2 * at
+                tall = jnp.concatenate([one(m), one(m + 1)], 0)
+                lanes = pl.ds(pl.multiple_of(at * (2 * block), 2 * block), 2 * block)
+                total = tall.T + alpha[0, :, lanes]
+                out[:, lanes] = jnp.where(kept, total, jnp.float32(0.0))
             return carry
 
-        lax.fori_loop(0, width // (2 * block), pair, 0)
+        lax.fori_loop(0, pairs // together, some_pairs, 0)
 
 
 def beta_call(own, partner, alpha, left, right, entries, types, keep, block):
@@ -184,11 +211,14 @@
     )(keep, entries, types, *own, *partner, alpha, left, right)
 
 
-def exchange_kernel(groups, parts, *refs):
-    own, alpha = refs[:parts], refs[parts]
-    refs = refs[parts + 1 :]
+def exchange_kernel(groups, parts, chunk, a_high, a_low, coeffs, *refs):
+    own = refs[:parts]
+    refs = refs[parts:]
     own_in, partner_in, alpha_in = refs[:parts], refs[parts : 2 * parts], refs[2 * parts]
-    own_send, own_recv, far_send, far_recv, alpha_send, alpha_recv, local = refs[2 * parts + 1 :]
+    own_send, own_recv, far_send, far_recv, alpha_send, alpha_recv, local = refs[
+        2 * parts + 1 : 2 * parts + 8
+    ]
+    held, alpha, held_high, held_low = refs[2 * parts + 8 :]
     cls, me = lax.axis_index("cls"), lax.axis_index("col")
     other = cls ^ 1
 
@@ -232,15 +262,28 @@
     far_copies = [[far(p, x) for x in range(groups)] for p in range(parts)]
     local_copies = [
         pltpu.make_async_copy(own[p].at[me], own_in[p].at[me], local.at[p]) for p in range(parts)
-    ] + [pltpu.make_async_copy(alpha.at[me], alpha_in.at[me], local.at[parts])]
+    ]
+    alpha_local = pltpu.make_async_copy(alpha.at[me], alpha_in.at[me], local.at[parts])
+    loading = [
+        pltpu.make_async_copy(source, target, local.at[parts + 1 + nth])
+        for nth, (source, target) in enumerate(
+            [(coeffs, held), (a_high, held_high), (a_low, held_low)]
+        )
+    ]
     waves = own_copies + [alpha_copies]
 
+    for copy in loading:
+        copy.start()
     for part in range(parts):
         far_copies[part][0].start()
     for copy in waves[0] + waves[1]:
         copy.start()
     for copy in local_copies:
         copy.start()
+    for copy in loading:
+        copy.wait()
+    alpha_product(chunk, held, held_high, held_low, alpha)
+    alpha_local.start()
     for part in range(parts):
         for at, copy in enumerate(own_copies[part]):
             copy.wait_recv()
@@ -253,30 +296,41 @@
     for copies in far_copies:
         for copy in copies:
             copy.wait_recv()
-    for copy in local_copies:
+    for copy in local_copies + [alpha_local]:
         copy.wait()
     for copies in waves + far_copies:
         for copy in copies:
             copy.wait_send()
 
 
-def exchange_call(own, alpha):
-    groups = alpha.shape[0]
+def exchange_call(own, coeffs_t, a_high, a_low):
+    groups, piece, width = own[0].shape
     parts = len(own)
+    capacity = parts * piece
     shape = lambda x: jax.ShapeDtypeStruct(x.shape, x.dtype)
-    outs = [shape(x) for x in own] * 2 + [shape(alpha)]
+    alpha = jax.ShapeDtypeStruct((groups, capacity, width), jnp.float32)
+    outs = [shape(x) for x in own] * 2 + [alpha]
     dma = pltpu.SemaphoreType.DMA
+    anywhere = pl.BlockSpec(memory_space=pl.ANY)
     got = pl.pallas_call(
-        functools.partial(exchange_kernel, groups, parts),
+        functools.partial(exchange_kernel, groups, parts, column_chunk(width)),
         out_shape=outs,
-        in_specs=[pl.BlockSpec(memory_space=pl.ANY)] * (parts + 1),
-        out_specs=[pl.BlockSpec(memory_space=pl.ANY)] * len(outs),
-        scratch_shapes=[dma((parts, groups))] * 4 + [dma((groups,))] * 2 + [dma((parts + 1,))],
+        in_specs=[anywhere] * (parts + 3),
+        out_specs=[anywhere] * len(outs),
+        scratch_shapes=[dma((parts, groups))] * 4
+        + [dma((groups,))] * 2
+        + [dma((parts + 4,))]
+        + [
+            pltpu.VMEM(coeffs_t.shape, jnp.float32),
+            pltpu.VMEM(alpha.shape, jnp.float32),
+            pltpu.VMEM(a_high.shape, jnp.bfloat16),
+            pltpu.VMEM(a_low.shape, jnp.bfloat16),
+        ],
         compiler_params=pltpu.CompilerParams(
             collective_id=0, has_side_effects=True, vmem_limit_bytes=VMEM_BYTES
         ),
         name="exchange",
-    )(*own, alpha)
+    )(a_high, a_low, coeffs_t, *own)
     return got[:parts], got[parts : 2 * parts], got[2 * parts]
 
 
@@ -297,28 +351,15 @@
 
 
 def alpha_weights(alpha_table, block):
-    tables = alpha_table.reshape(-1, block, block)
-    return weights(jnp.pad(tables, ((0, 1), (0, 0), (0, 0))))
+    tables = jnp.pad(alpha_table.reshape(-1, block, block), ((0, 1), (0, 0), (0, 0)))
+    return (
+        jnp.pad(tables, ((0, 0), (0, 0), (0, block))),
+        jnp.pad(tables, ((0, 0), (0, 0), (block, 0))),
+    )
 
 
 def beta_weights(beta_table, block):
     return weights(jnp.transpose(beta_table.reshape(-1, block, block), (0, 2, 1)))
-
-
-def alpha_call(coeffs_t, starts, alpha_table, alpha_blocks, alpha_types, groups, capacity, block):
-    rows = coeffs_t.shape[1]
-    types = alpha_entries(alpha_blocks, alpha_types, alpha_table.shape[0])
-    return slots_call(
-        functools.partial(alpha_kernel, block),
-        coeffs_t,
-        (starts, types),
-        alpha_weights(alpha_table, block),
-        [pltpu.VMEM((rows, rows), jnp.bfloat16)] * 2,
-        groups,
-        capacity,
-        1,
-        "alpha_slots",
-    )[0]
 
 
 def even_wide(x, block):
@@ -346,13 +387,12 @@
     starts = (jnp.cumsum(row_counts) - row_counts).astype(jnp.int32)
     keep = lax.dynamic_slice(row_counts, (lax.axis_index("col"),), (1,))
 
-    coeff_slots = slots_call(
-        coeff_kernel, coeffs_t, (starts,), (), (), groups, capacity, ROW_PARTS, "coeff_slots"
-    )
-    alpha_slots = alpha_call(
-        coeffs_t, starts, alpha_table, alpha_blocks, alpha_types, groups, capacity, block
-    )
-    own, partner, alpha = exchange_call(coeff_slots, alpha_slots)
+    coeff_slots = slots_call(coeffs_t, starts, groups, capacity, ROW_PARTS)
+    types = alpha_entries(alpha_blocks, alpha_types, alpha_table.shape[0])
+    a_high, a_low = alpha_rows_call(
+        starts, types, *alpha_weights(alpha_table, block), rows, groups, capacity, block
+    )
+    own, partner, alpha = exchange_call(coeff_slots, coeffs_t, a_high, a_low)
     left, right = beta_weights(beta_table, block)
     wide = lambda x: even_wide(x, block)
     return beta_call(

time: 323 us -> 301 us (0.932)
  Pallas kernels: 304 us -> 283 us
    pallas_call x1, Pallas kernels: 65.1 us -> 50.2 us  [beta_call(): pl.pallas_call(functools.partial(beta_kernel, groups, parts, block), out_...]
    pallas_call x3, Pallas kernels: 239 us -> 233 us  [the longest x1 214 us: exchange_call(): pl.pallas_call(functools.partial(exchange_kernel, groups, parts, column_c...]
where the time goes in v3:
time: 301 us
  Pallas kernels  283 us (94%)
  local copies, waits for them, and re-layouts  15.4 us (5%)
    pallas_call x1, Pallas kernels, exchange_call(): pl.pallas_call(functools.partial(exchange_kernel, groups, parts, column_c...  214 us
    pallas_call x1, Pallas kernels, beta_call(): pl.pallas_call(functools.partial(beta_kernel, groups, parts, block), out_...  50.2 us
    pallas_call x1, Pallas kernels, alpha_rows_call(): pl.pallas_call(functools.partial(alpha_rows_kernel, block), out_shape=[ou...  10 us
    pallas_call x1, Pallas kernels, slots_call(): pl.pallas_call(coeff_kernel, out_shape=[out] * parts, grid=(width // chun...  8.48 us

profile of v3, /device:TPU:0, one launch (start us, length us, event | category | flops | bytes accessed | tf_op | source)
XLA Modules:
  0.0 300.7 jit_solution(9506803509675663264)
XLA Ops:
  0.0 2.0 reshape.49
  2.0 0.3 pad.20
  2.3 0.0 copy-start.5
  2.3 0.0 copy-start.1
  2.3 0.0 copy-start.4
  2.3 2.7 fusion.2
  5.1 0.0 copy-done.5
  5.1 0.2 reduce-window.9
  5.2 0.5 bitcast_subtract_fusion.starts
  5.8 0.0 copy-done.1
  5.8 0.0 copy-done.4
  5.8 0.1 select_reduce_fusion
  5.9 0.1 fusion.1
  6.1 0.6 select_n.18.types
  6.7 10.0 %alpha_rows.1 = (bf16[8,192,1024]{2,1,0:T(8,128)(2,1)}, bf16[8,192,1024]{2,1,0:T(8,128)(2,1)}) custom-call(s32[8]{0:T(128)} %bitcast_subtract_fusion.starts, s32[256]{0:T(256)} %select_n.18.types, f32[65,64,128]{2,1,0:T(8,128)} %get-tuple-element.30.left, f32[65,64,128]{2,1,0:T(8,128)} %get-tuple-element.29.right), custom_call_target="tpu_custom_call" | custom-call | tf_op jit(solution)/shard_map/alpha_rows/pallas_call | solution.py:78
  16.7 8.5 %coeff_slots.1 = (f32[8,64,1536]{2,1,0:T(8,128)}, f32[8,64,1536]{2,1,0:T(8,128)}, f32[8,64,1536]{2,1,0:T(8,128)}) custom-call(s32[8]{0:T(128)} %bitcast_subtract_fusion.starts, f32[1536,1024]{1,0:T(8,128)} %coeffs.3), custom_call_target="tpu_custom_call" | custom-call | tf_op jit(solution)/shard_map/coeff_slots/pallas_call | solution.py:110
  25.2 214.4 %exchange.1 = (f32[8,64,1536]{2,1,0:T(8,128)}, f32[8,64,1536]{2,1,0:T(8,128)}, f32[8,64,1536]{2,1,0:T(8,128)}, f32[8,64,1536]{2,1,0:T(8,128)}, f32[8,64,1536]{2,...) custom-call(bf16[8,192,1024]{2,1,0:T(8,128)(2,1)} %get-tuple-element.17.a_high, ...), custom_call_target="tpu_custom_call" | custom-call | tf_op jit(solution)/shard_map/exchange/pallas_call | solution.py:315
  239.6 0.7 dynamic_slice.3.keep
  240.2 0.0 copy-done
  240.2 2.2 reshape.50
  242.4 1.9 copy.14
  244.3 0.6 reduce-precision_convert_fusion
  244.9 0.6 pad_maximum_fusion
  245.5 0.0 copy-start.2
  245.5 0.0 copy-start.3
  245.5 3.4 %fusion.3 = (bf16[64,128,128]{2,1,0:T(8,128)(2,1)}, bf16[64,128,128]{2,1,0:T(8,128)(2,1)}) fusion(bf16[64,128,64]{2,1,0:T(8,128)(2,1)S(1)} %pad_maximum_fusion), kind=kLoop, calls=%fused_computation.10 | loop fusion | bytes 5242880 | tf_op jit(solution)/shard_map/jit(_pad)/pad | solution.py:349
  248.9 0.0 copy-done.2
  248.9 0.1 copy.12
  249.0 0.7 reshape.45.entries
  249.7 0.1 copy.13
  249.8 0.7 reshape.46.types
  250.5 50.2 %beta_sum.1 = f32[192,12288]{1,0:T(8,128)} custom-call(s32[1]{0:T(128)} %dynamic_slice.3.keep, s32[2304]{0:T(1024)} %reshape.45.entries, s32[2304]{0:T(1024)} %reshape.46.types, f32[8,64,1536]{2,1,0:T(8,128)} %get-tuple-element.22.rest_0_, f32[8,64,1536]{2,1,0:T(8,128)} %get-tuple-element.23.rest_1_, f32[8,64,1536]{2,1,0:T(8,128)} %get-tuple-element.24.rest_2_, ...), custom_call_target="tpu_custom_call" | custom-call | tf_op jit(solution)/shard_map/beta_sum/pallas_call | solution.py:197
  (3 shorter events, 0.0 us)
Async XLA Ops:
  2.3 2.8 copy-start.5
  2.3 3.5 %copy-start.1 = (s32[16,16]{1,0:T(8,128)S(1)}, s32[16,16]{1,0:T(8,128)}, u32[]{:S(2)}) copy-start(s32[16,16]{1,0:T(8,128)} %param.10) | copy-start | bytes 3076
  2.3 3.5 %copy-start.4 = (s32[16,16]{1,0:T(8,128)S(1)}, s32[16,16]{1,0:T(8,128)}, u32[]{:S(2)}) copy-start(s32[16,16]{1,0:T(8,128)} %param.11) | copy-start | bytes 3076
  25.2 215.1 %copy-start = (f32[64,4096]{1,0:T(8,128)S(1)}, f32[64,4096]{1,0:T(8,128)}, u32[]{:S(2)}) copy-start(f32[64,4096]{1,0:T(8,128)} %param.12) | copy-start | bytes 3145732
  245.5 3.4 %copy-start.2 = (s32[192,12]{0,1:T(8,128)S(1)}, s32[192,12]{0,1:T(8,128)}, u32[]{:S(2)}) copy-start(s32[192,12]{0,1:T(8,128)} %param.13) | copy-start | bytes 27652
  245.5 4.2 %copy-start.3 = (s32[192,12]{0,1:T(8,128)S(1)}, s32[192,12]{0,1:T(8,128)}, u32[]{:S(2)}) copy-start(s32[192,12]{0,1:T(8,128)} %param.14) | copy-start | bytes 27652
